TPU v7x, 32 devices: a whole 2x2x4 slice. The times are simulated.
32 devices in a mesh: rows: 2 (over y), cols: 4 (over z), layers: 4 (over x, core).
Axes of the slice: x: 2, y: 2, z: 4, core: 2. Of those that a mesh axis runs over, the one named last changes fastest.
Arguments:
- y_blocks: bfloat16 [96, 16, 128, 128], P('rows', ('cols', 'layers')), may hold values from -1 to 1
- y_cols: int32 [96, 16], P('rows', ('cols', 'layers')), may hold values from 0 to 95, as said below
- prod_blocks: bfloat16 [96, 16, 128, 128], P('rows', ('cols', 'layers')), may hold values from -1 to 1
- prod_cols: int32 [96, 16], P('rows', ('cols', 'layers')), may hold values from 0 to 95, as said below
- out_cols: int32 [96, 16, 2], P('rows', ('cols', 'layers')), may hold values from 0 to 95, as said below
Outputs:
- y_next: bfloat16 [96, 16, 2, 128, 128], P('rows', ('cols', 'layers'))
Inputs may be any that keep to these rules, and one draw needn't show every extreme that they name: y_cols[i, t] lies in [t * 6, (t + 1) * 6): each block row of Y holds exactly one block in each range of 6 block columns. prod_cols[k, t] lies in [t * 6, (t + 1) * 6): each block row of M holds exactly one block in each range of 6 block columns. out_cols[i, t, :] are 2 distinct block columns in [t * 6, (t + 1) * 6), one of them equal to y_cols[i, t].
All inputs are finite; a program needn't handle non-finite values.
Results may differ from a plain program's by a relative error of at most 0.001.
Values may be sent and summed in bfloat16 or wider, within the bound.
A program may use at most 128 MiB of HBM per device.

v0:
```python
import jax
import jax.numpy as jnp
from jax import lax
from jax.sharding import PartitionSpec as P

TILE_COLS = 6


def partial_products(
    running, shard_piece, lookup, lookup_cols, target_cols, layer_count, tile_cols
):
    left_all, left_cols = shard_piece
    block_rows, piece_len = left_cols.shape
    tile_count = target_cols.shape[1]
    outputs = block_rows * tile_count
    group_size = 1
    while group_size * 2 <= max(1, 64 // outputs) and piece_len % (group_size * 2) == 0:
        group_size = group_size * 2

    def advance(position, summed):
        offset = position * group_size
        left_blocks = lax.dynamic_slice_in_dim(left_all, offset, group_size, 1)
        inner_cols = lax.dynamic_slice_in_dim(left_cols, offset, group_size, 1)
        lookup_rows = inner_cols // (layer_count * tile_cols) * tile_cols + inner_cols % tile_cols
        right_blocks = lookup[lookup_rows]
        right_cols = lookup_cols[lookup_rows]
        present = (right_cols[:, :, :, None] == target_cols[:, None, :, :]).astype(jnp.float32)
        products = jnp.einsum(
            "igab,igtbc->igtac", left_blocks, right_blocks, preferred_element_type=jnp.float32
        )
        weighted = jnp.sum(products[:, :, :, None] * present[..., None, None], axis=1)
        return summed + weighted

    return lax.fori_loop(0, piece_len // group_size, advance, running)


def shards(y_blocks, y_cols, prod_blocks, prod_cols, out_cols):
    block_rows = y_blocks.shape[0]
    block_size = y_blocks.shape[2]
    out_width = out_cols.shape[2]
    tile_cols = TILE_COLS
    lookup, lookup_cols = (
        lax.all_gather(prod_blocks, "rows", axis=0, tiled=True),
        lax.all_gather(prod_cols, "rows", axis=0, tiled=True),
    )
    initial = jnp.zeros((block_rows, 1, out_width, block_size, block_size), jnp.float32)
    summed = partial_products(
        initial,
        (
            lax.all_gather(y_blocks, ("cols", "layers"), axis=1, tiled=True),
            lax.all_gather(y_cols, ("cols", "layers"), axis=1, tiled=True),
        ),
        lookup,
        lookup_cols,
        out_cols,
        1,
        tile_cols,
    )
    matches = out_cols == y_cols[:, :, None]
    own_blocks = jnp.where(matches[..., None, None], y_blocks[:, :, None].astype(jnp.float32), 0.0)
    updated = 1.5 * own_blocks - 0.5 * summed
    return updated.astype(jnp.bfloat16)


def solution(mesh):
    placed = (
        P("rows", ("cols", "layers"), None, None),
        P("rows", ("cols", "layers")),
        P("rows", ("cols", "layers"), None, None),
        P("rows", ("cols", "layers")),
        P("rows", ("cols", "layers"), None),
    )
    return jax.shard_map(
        shards,
        mesh=mesh,
        in_specs=placed,
        out_specs=P("rows", ("cols", "layers"), None, None, None),
        check_vma=False,
    )
```

profile of v0, /device:TPU:0, one launch (start us, length us, event | category | flops | bytes accessed | tf_op | source)
XLA Modules:
  0.0 463.2 jit_solution(1917132173694149642)
XLA Ops:
  9.6 5.2 %all-reduce = s32[96]{0:T(128)S(1)} all-reduce(s32[96]{0:T(128)S(1)} %bitcast_dynamic-update-slice_fusion), channel_id=1, replica_groups=mesh['rows'=2,'cols'=4,'layers'=4] {'rows'}, use_global_device_ids=true, to_apply=%add | all-reduce | flops 96 | bytes 768
  14.8 22.0 %all-gather = s32[16,1,48]{2,1,0:T(1,128)S(1)} all-gather(s32[1,1,48]{2,1,0:T(1,128)S(1)} %bitcast.51), channel_id=1, replica_groups=mesh['rows'=2,'cols'=4,'layers'=4] {'cols','layers'}, dimensions={0}, use_global_device_ids=true | all-gather | bytes 3264 | tf_op jit(solution)/shard_map/all_gather | solution.py:51
  38.8 17.8 %all-gather.4.cloned.1.call-done = bf16[96,1,128,128]{3,2,1,0:T(8,128)(2,1)} async-done(((bf16[48,1,128,128]{3,2,1,0:T(8,128)(2,1)}), bf16[96,1,128,128]{3,2,1,0:T(8,128)(2,1)}) %all-gather.4.cloned.1.call-update) | async-done | bytes 3145744 | tf_op jit(solution)/shard_map/all_gather | solution.py:43
  56.6 130.2 %all-gather.6.cloned.1.call-done = bf16[48,16,128,128]{3,2,0,1:T(8,128)(2,1)} async-done(((bf16[48,1,128,128]{3,2,0,1:T(8,128)(2,1)}), bf16[48,16,128,128]{3,2,0,1:T(8,128)(2,1)}) %all-gather.6.cloned.1.call-update) | async-done | bytes 25165840 | tf_op jit(solution)/shard_map/all_gather | solution.py:50
  186.8 264.0 %while.16 = (s32[]{:T(128)}, f32[48,1,2,128,128]{4,3,2,1,0:T(8,128)}, s32[48,16]{0,1:T(8,128)S(1)}, bf16[96,1,128,128]{3,2,1,0:T(8,128)(2,1)}, bf16[48,16,128,12...) while((s32[]{:T(128)}, ...), condition=%wide.region_1.2_spmd.clone, body=%wide.region_0.1_spmd.clone.sunk | while | flops 206047216 | bytes 31465452 | solution.py:34
  189.6 4.3 convolution_bitcast_fusion.2
  211.1 6.3 %select_add_fusion.2 = f32[48,1,2,128,128]{4,3,2,1,0:T(8,128)} fusion(f32[48,1,2,128,128]{4,3,2,1,0:T(8,128)} %get-tuple-element.276, f32[48,2]{1,0:T(8,128)S(1)} %copy.24, f32[48,128,128]{2,1,0:T(8,128)S(1)} %copy.25, pred[]{:T(512)S(6)} %compare.3), kind=kLoop, calls=%fused_computation.2.clone.1 | loop fusion | flops 4718592 | bytes 15729025 | tf_op jit(solution)/shard_map/while/body/eval_jaxpr/add | solution.py:32
  227.8 6.3 %select_add_fusion.2 = f32[48,1,2,128,128]{4,3,2,1,0:T(8,128)} fusion(f32[48,1,2,128,128]{4,3,2,1,0:T(8,128)} %get-tuple-element.276, f32[48,2]{1,0:T(8,128)S(1)} %copy.24, f32[48,128,128]{2,1,0:T(8,128)S(1)} %copy.25, pred[]{:T(512)S(6)} %compare.3), kind=kLoop, calls=%fused_computation.2.clone.1 | loop fusion | flops 4718592 | bytes 15729025 | tf_op jit(solution)/shard_map/while/body/eval_jaxpr/add | solution.py:32
  236.8 4.3 convolution_bitcast_fusion.2
  244.4 6.3 %select_add_fusion.2 = f32[48,1,2,128,128]{4,3,2,1,0:T(8,128)} fusion(f32[48,1,2,128,128]{4,3,2,1,0:T(8,128)} %get-tuple-element.276, f32[48,2]{1,0:T(8,128)S(1)} %copy.24, f32[48,128,128]{2,1,0:T(8,128)S(1)} %copy.25, pred[]{:T(512)S(6)} %compare.3), kind=kLoop, calls=%fused_computation.2.clone.1 | loop fusion | flops 4718592 | bytes 15729025 | tf_op jit(solution)/shard_map/while/body/eval_jaxpr/add | solution.py:32
  261.1 6.3 %select_add_fusion.2 = f32[48,1,2,128,128]{4,3,2,1,0:T(8,128)} fusion(f32[48,1,2,128,128]{4,3,2,1,0:T(8,128)} %get-tuple-element.276, f32[48,2]{1,0:T(8,128)S(1)} %copy.24, f32[48,128,128]{2,1,0:T(8,128)S(1)} %copy.25, pred[]{:T(512)S(6)} %compare.3), kind=kLoop, calls=%fused_computation.2.clone.1 | loop fusion | flops 4718592 | bytes 15729025 | tf_op jit(solution)/shard_map/while/body/eval_jaxpr/add | solution.py:32
  270.2 4.3 convolution_bitcast_fusion.2
  277.8 6.3 %select_add_fusion.2 = f32[48,1,2,128,128]{4,3,2,1,0:T(8,128)} fusion(f32[48,1,2,128,128]{4,3,2,1,0:T(8,128)} %get-tuple-element.276, f32[48,2]{1,0:T(8,128)S(1)} %copy.24, f32[48,128,128]{2,1,0:T(8,128)S(1)} %copy.25, pred[]{:T(512)S(6)} %compare.3), kind=kLoop, calls=%fused_computation.2.clone.1 | loop fusion | flops 4718592 | bytes 15729025 | tf_op jit(solution)/shard_map/while/body/eval_jaxpr/add | solution.py:32
  294.5 6.3 %select_add_fusion.2 = f32[48,1,2,128,128]{4,3,2,1,0:T(8,128)} fusion(f32[48,1,2,128,128]{4,3,2,1,0:T(8,128)} %get-tuple-element.276, f32[48,2]{1,0:T(8,128)S(1)} %copy.24, f32[48,128,128]{2,1,0:T(8,128)S(1)} %copy.25, pred[]{:T(512)S(6)} %compare.3), kind=kLoop, calls=%fused_computation.2.clone.1 | loop fusion | flops 4718592 | bytes 15729025 | tf_op jit(solution)/shard_map/while/body/eval_jaxpr/add | solution.py:32
  311.1 6.3 %select_add_fusion.2 = f32[48,1,2,128,128]{4,3,2,1,0:T(8,128)} fusion(f32[48,1,2,128,128]{4,3,2,1,0:T(8,128)} %get-tuple-element.276, f32[48,2]{1,0:T(8,128)S(1)} %copy.24, f32[48,128,128]{2,1,0:T(8,128)S(1)} %copy.25, pred[]{:T(512)S(6)} %compare.3), kind=kLoop, calls=%fused_computation.2.clone.1 | loop fusion | flops 4718592 | bytes 15729025 | tf_op jit(solution)/shard_map/while/body/eval_jaxpr/add | solution.py:32
  327.8 6.3 %select_add_fusion.2 = f32[48,1,2,128,128]{4,3,2,1,0:T(8,128)} fusion(f32[48,1,2,128,128]{4,3,2,1,0:T(8,128)} %get-tuple-element.276, f32[48,2]{1,0:T(8,128)S(1)} %copy.24, f32[48,128,128]{2,1,0:T(8,128)S(1)} %copy.25, pred[]{:T(512)S(6)} %compare.3), kind=kLoop, calls=%fused_computation.2.clone.1 | loop fusion | flops 4718592 | bytes 15729025 | tf_op jit(solution)/shard_map/while/body/eval_jaxpr/add | solution.py:32
  344.5 6.3 %select_add_fusion.2 = f32[48,1,2,128,128]{4,3,2,1,0:T(8,128)} fusion(f32[48,1,2,128,128]{4,3,2,1,0:T(8,128)} %get-tuple-element.276, f32[48,2]{1,0:T(8,128)S(1)} %copy.24, f32[48,128,128]{2,1,0:T(8,128)S(1)} %copy.25, pred[]{:T(512)S(6)} %compare.3), kind=kLoop, calls=%fused_computation.2.clone.1 | loop fusion | flops 4718592 | bytes 15729025 | tf_op jit(solution)/shard_map/while/body/eval_jaxpr/add | solution.py:32
  361.1 6.3 %select_add_fusion.2 = f32[48,1,2,128,128]{4,3,2,1,0:T(8,128)} fusion(f32[48,1,2,128,128]{4,3,2,1,0:T(8,128)} %get-tuple-element.276, f32[48,2]{1,0:T(8,128)S(1)} %copy.24, f32[48,128,128]{2,1,0:T(8,128)S(1)} %copy.25, pred[]{:T(512)S(6)} %compare.3), kind=kLoop, calls=%fused_computation.2.clone.1 | loop fusion | flops 4718592 | bytes 15729025 | tf_op jit(solution)/shard_map/while/body/eval_jaxpr/add | solution.py:32
  377.8 6.3 %select_add_fusion.2 = f32[48,1,2,128,128]{4,3,2,1,0:T(8,128)} fusion(f32[48,1,2,128,128]{4,3,2,1,0:T(8,128)} %get-tuple-element.276, f32[48,2]{1,0:T(8,128)S(1)} %copy.24, f32[48,128,128]{2,1,0:T(8,128)S(1)} %copy.25, pred[]{:T(512)S(6)} %compare.3), kind=kLoop, calls=%fused_computation.2.clone.1 | loop fusion | flops 4718592 | bytes 15729025 | tf_op jit(solution)/shard_map/while/body/eval_jaxpr/add | solution.py:32
  394.5 6.3 %select_add_fusion.2 = f32[48,1,2,128,128]{4,3,2,1,0:T(8,128)} fusion(f32[48,1,2,128,128]{4,3,2,1,0:T(8,128)} %get-tuple-element.276, f32[48,2]{1,0:T(8,128)S(1)} %copy.24, f32[48,128,128]{2,1,0:T(8,128)S(1)} %copy.25, pred[]{:T(512)S(6)} %compare.3), kind=kLoop, calls=%fused_computation.2.clone.1 | loop fusion | flops 4718592 | bytes 15729025 | tf_op jit(solution)/shard_map/while/body/eval_jaxpr/add | solution.py:32
  411.2 6.3 %select_add_fusion.2 = f32[48,1,2,128,128]{4,3,2,1,0:T(8,128)} fusion(f32[48,1,2,128,128]{4,3,2,1,0:T(8,128)} %get-tuple-element.276, f32[48,2]{1,0:T(8,128)S(1)} %copy.24, f32[48,128,128]{2,1,0:T(8,128)S(1)} %copy.25, pred[]{:T(512)S(6)} %compare.3), kind=kLoop, calls=%fused_computation.2.clone.1 | loop fusion | flops 4718592 | bytes 15729025 | tf_op jit(solution)/shard_map/while/body/eval_jaxpr/add | solution.py:32
  427.8 6.3 %select_add_fusion.2 = f32[48,1,2,128,128]{4,3,2,1,0:T(8,128)} fusion(f32[48,1,2,128,128]{4,3,2,1,0:T(8,128)} %get-tuple-element.276, f32[48,2]{1,0:T(8,128)S(1)} %copy.24, f32[48,128,128]{2,1,0:T(8,128)S(1)} %copy.25, pred[]{:T(512)S(6)} %compare.3), kind=kLoop, calls=%fused_computation.2.clone.1 | loop fusion | flops 4718592 | bytes 15729025 | tf_op jit(solution)/shard_map/while/body/eval_jaxpr/add | solution.py:32
  444.5 6.3 %select_add_fusion.2 = f32[48,1,2,128,128]{4,3,2,1,0:T(8,128)} fusion(f32[48,1,2,128,128]{4,3,2,1,0:T(8,128)} %get-tuple-element.276, f32[48,2]{1,0:T(8,128)S(1)} %copy.24, f32[48,128,128]{2,1,0:T(8,128)S(1)} %copy.25, pred[]{:T(512)S(6)} %compare.3), kind=kLoop, calls=%fused_computation.2.clone.1 | loop fusion | flops 4718592 | bytes 15729025 | tf_op jit(solution)/shard_map/while/body/eval_jaxpr/add | solution.py:32
  450.8 5.5 %subtract_convert_fusion = bf16[48,1,2,128,128]{4,3,2,1,0:T(8,128)(2,1)} fusion(f32[48,1,2,128,128]{4,3,2,1,0:T(8,128)} %get-tuple-element.184, f32[48,128,128]{2,1,0:T(8,128)} %bitcast_convert_fusion, pred[48,2]{1,0:T(8,128)(4,1)S(1)} %copy.19), kind=kLoop, calls=%fused_computation.14 | loop fusion | flops 7864320 | bytes 12583008 | tf_op jit(solution)/shard_map/convert_element_type | solution.py:62
  (147 shorter events, 160.4 us)
Async XLA Ops:
  6.5 1.7 copy-start.4
  6.5 30.2 %copy-start = (bf16[48,1,128,128]{3,2,1,0:T(8,128)(2,1)S(1)}, bf16[48,1,128,128]{3,2,1,0:T(8,128)(2,1)}, u32[]{:S(2)}) copy-start(bf16[48,1,128,128]{3,2,1,0:T(8,128)(2,1)} %param.7) | copy-start | bytes 4718596
  6.5 1.5 copy-start.1
  6.5 1.5 copy-start.2
  6.5 2.9 copy-start.3
  6.5 50.0 %all-gather.4.cloned.1.call-start = ((), (), s32[]{:S(2)}) async-start(), calls=%async_computation | async-start | bytes 4718592 | tf_op jit(solution)/shard_map/all_gather | solution.py:43
  7.3 179.5 %all-gather.6.cloned.1.call-start = ((), (), s32[]{:S(2)}) async-start(), calls=%async_computation.1 | async-start | bytes 26738688 | tf_op jit(solution)/shard_map/all_gather | solution.py:50
Sparse Core Ops, SparseCore 0:
  8.9 47.6 all-gather.3
  58.2 128.5 all-gather.5
where the time goes:
time: 465 us; the launch traced here: 463 us
  waiting for transfers between devices  149 us (32%)
  other arithmetic  106 us (23%)
  local copies, waits for them, and re-layouts  96.5 us (21%)
  matrix products  69.3 us (15%)
  blocking collectives  27.2 us (6%)
  between operations  14.1 us (3%)
    all_gather x1, waiting for transfers between devices, shards(): lax.all_gather(y_blocks, ('cols', 'layers'), axis=1, tiled=True)  130 us
    add x16, other arithmetic, advance(): return summed + weighted  98 us
    dot_general x16, matrix products, advance(): jnp.einsum('igab,igtbc->igtac', left_blocks, right_blocks, preferred_elem...  69.3 us
    gather x16, local copies, waits for them, and re-layouts, advance(): right_blocks = lookup[lookup_rows]  43.8 us
    mul x16, local copies, waits for them, and re-layouts, advance(): products[:, :, :, None] * present[..., None, None]  38 us
    all_gather x1, blocking collectives, shards(): lax.all_gather(y_cols, ('cols', 'layers'), axis=1, tiled=True)  22 us
    all_gather x1, waiting for transfers between devices, shards(): lax.all_gather(prod_blocks, 'rows', axis=0, tiled=True)  17.8 us
    gather x16, local copies, waits for them, and re-layouts, advance(): right_cols = lookup_cols[lookup_rows]  12.4 us
  transfers between devices with their start and end apart: 2, of which 2 were waited for; matrix products, arithmetic and copies ran while one was open for 1% of the time, Pallas kernels for 0%

commit v1 on v0

v1 whole, which is shorter than its diff:
```python
import functools

import jax
import jax.numpy as jnp
from jax import lax
from jax.experimental import pallas as pl
from jax.experimental.pallas import tpu as pltpu
from jax.sharding import PartitionSpec as P

TILE_COLS = 6
LANES = 128
MESH = pl.DeviceIdType.MESH
UP, DOWN, CROSS, SIBLING = range(4)


def kernel(
    row_count, col_count, y_ref, m_ref, ymeta_ref, pmeta_ref, ycols_ref, out_cols_ref, out_ref,
    yall, mall, acc, ymeta, pmeta, ytable, ptable,
    send_sem, recv_sem, msend_sem, mrecv_sem, row_send, row_recv, rmeta_send, rmeta_recv, local_sem,
):
    rows = y_ref.shape[0]
    half = rows // 2
    r, z, l = lax.axis_index("rows"), lax.axis_index("cols"), lax.axis_index("layers")
    cross = lax.rem(l + 2, 4)
    sibling = l + 1 - 2 * lax.rem(l, 2)
    cross_sibling = lax.rem(sibling + 2, 4)
    paired = z + 1 - 2 * lax.rem(z, 2)
    targets = {UP: (r, z + 1, l), DOWN: (r, z - 1, l), CROSS: (r, z, cross), SIBLING: (r, z, sibling)}

    own_copies = [
        pltpu.make_async_copy(y_ref, yall.at[z, l], local_sem.at[0]),
        pltpu.make_async_copy(m_ref, mall.at[pl.ds(r * rows, rows)], local_sem.at[1]),
        pltpu.make_async_copy(ymeta_ref, ymeta.at[z, l], local_sem.at[2]),
        pltpu.make_async_copy(pmeta_ref, pmeta.at[r], local_sem.at[3]),
    ]
    for copy in own_copies:
        copy.start()

    barrier = pltpu.get_barrier_semaphore()

    def greet(device):
        pl.semaphore_signal(barrier, inc=1, device_id=device, device_id_type=MESH)

    greet(targets[CROSS])
    greet(targets[SIBLING])
    for step in range(1, row_count):
        greet((lax.rem(r + step, row_count), z, l))

    @pl.when(z + 1 < col_count)
    def _():
        greet(targets[UP])

    @pl.when(z > 0)
    def _():
        greet(targets[DOWN])

    line_peers = jnp.where(z > 0, 1, 0) + jnp.where(z + 1 < col_count, 1, 0)
    pl.semaphore_wait(barrier, 1 + row_count + line_peers)

    for copy in own_copies:
        copy.wait()

    def chunk_copy(way, at, tile, part, device):
        return pltpu.make_async_remote_copy(
            src_ref=yall.at[at, tile, pl.ds(part * half, half)],
            dst_ref=yall.at[at, tile, pl.ds(part * half, half)],
            send_sem=send_sem.at[way, at, tile, part],
            recv_sem=recv_sem.at[at, tile, part],
            device_id=device,
            device_id_type=MESH,
        )

    def meta_copy(way, at, tile, device):
        return pltpu.make_async_remote_copy(
            src_ref=ymeta.at[at, tile],
            dst_ref=ymeta.at[at, tile],
            send_sem=msend_sem.at[way, at, tile],
            recv_sem=mrecv_sem.at[at, tile],
            device_id=device,
            device_id_type=MESH,
        )

    def send(way, at, tile, part, start, device=None):
        device = targets[way] if device is None else device
        chunk = chunk_copy(way, at, tile, part, device)
        if start:
            chunk.start()
        else:
            chunk.wait_send()

        @pl.when(part == 0)
        def _():
            meta = meta_copy(way, at, tile, device)
            if start:
                meta.start()
            else:
                meta.wait_send()

    def arrive(at, tile, part):
        chunk_copy(SIBLING, at, tile, part, targets[SIBLING]).wait_recv()

        @pl.when(part == 0)
        def _():
            meta_copy(SIBLING, at, tile, targets[SIBLING]).wait_recv()

    def origins(step):
        away, part = step // 2, lax.rem(step, 2)
        return away, part, ((z - away, z - away >= 0), (z + away, jnp.logical_and(z + away < col_count, away > 0)))

    def line_step(step, start):
        away, part, sides = origins(step)
        for side, (at, valid) in enumerate(sides):
            @pl.when(valid)
            def _():
                if start:
                    @pl.when(away > 0)
                    def _():
                        arrive(at, l, part)

                if side == 0:
                    @pl.when(z + 1 < col_count)
                    def _():
                        send(UP, at, l, part, start)

                @pl.when(jnp.logical_and(z > 0, (away == 0) if side == 0 else True))
                def _():
                    send(DOWN, at, l, part, start)

                @pl.when(jnp.logical_not(jnp.logical_and(at == paired, part == 1)))
                def _():
                    send(CROSS, at, l, part, start)

                send(SIBLING, at, l, part, start)

    def cross_step(step, start):
        away, part, sides = origins(step)
        for at, valid in sides:
            @pl.when(jnp.logical_and(valid, jnp.logical_not(jnp.logical_and(at == paired, part == 1))))
            def _():
                if start:
                    arrive(at, cross, part)
                send(SIBLING, at, cross, part, start)

    def compute(at, part):
        arrive(at, sibling, part)
        arrive(at, cross_sibling, part)

        @pl.when(part == 0)
        def _():
            table = pltpu.make_async_copy(ymeta.at[at], ytable.at[at], local_sem.at[0])
            table.start()
            table.wait()

        def one_row(j, carry):
            i = part * half + j
            wanted = [out_cols_ref[2 * i], out_cols_ref[2 * i + 1]]
            left, right = [], []
            for tile in range(4):
                left.append(yall[at, tile, i])
                first = TILE_COLS * (at * 4 + tile)
                inner = ytable[at, tile, 0, i]
                found = ptable[first // rows, 0, ytable[at, tile, 1, i]]
                right.append(jnp.concatenate(
                    [mall[jnp.where(found == want, inner, row_count * rows)] for want in wanted], axis=1
                ))
            acc[i] += jnp.dot(
                jnp.concatenate(left, axis=1), jnp.concatenate(right, axis=0),
                preferred_element_type=jnp.float32,
            )
            return carry

        lax.fori_loop(0, half, one_row, 0)

    def compute_step(step):
        away, part, sides = origins(step)
        for at, valid in sides:
            @pl.when(jnp.logical_and(valid, jnp.logical_not(jnp.logical_and(at == paired, part == 1))))
            def _():
                compute(at, part)

    def row_copies(other):
        device = (other, z, l)
        blocks = pltpu.make_async_remote_copy(
            src_ref=mall.at[pl.ds(r * rows, rows)],
            dst_ref=mall.at[pl.ds(r * rows, rows)],
            send_sem=row_send.at[other],
            recv_sem=row_recv.at[r],
            device_id=device,
            device_id_type=MESH,
        )
        meta = pltpu.make_async_remote_copy(
            src_ref=pmeta.at[r],
            dst_ref=pmeta.at[r],
            send_sem=rmeta_send.at[other],
            recv_sem=rmeta_recv.at[r],
            device_id=device,
            device_id_type=MESH,
        )
        return blocks, meta

    def row_arrivals(other):
        device = (other, z, l)
        blocks = pltpu.make_async_remote_copy(
            src_ref=mall.at[pl.ds(other * rows, rows)],
            dst_ref=mall.at[pl.ds(other * rows, rows)],
            send_sem=row_send.at[other],
            recv_sem=row_recv.at[other],
            device_id=device,
            device_id_type=MESH,
        )
        meta = pltpu.make_async_remote_copy(
            src_ref=pmeta.at[other],
            dst_ref=pmeta.at[other],
            send_sem=rmeta_send.at[other],
            recv_sem=rmeta_recv.at[other],
            device_id=device,
            device_id_type=MESH,
        )
        return blocks, meta

    def extra(start):
        send(UP, z, cross, 1, start, (r, paired, l))

    last = 2 * col_count

    def advance(step, carry):
        @pl.when(step < last)
        def _():
            line_step(step, True)

        @pl.when(step == 0)
        def _():
            for other in range(1, row_count):
                for copy in row_copies(lax.rem(r + other, row_count)):
                    copy.start()
            mall[row_count * rows] = jnp.zeros(mall.shape[1:], mall.dtype)

            def begin(i, carry):
                own = yall[z, l, i].astype(jnp.float32)
                mine = ycols_ref[i]
                for w in range(2):
                    scale = jnp.where(out_cols_ref[2 * i + w] == mine, -3.0, 0.0)
                    acc[i, :, w * LANES:(w + 1) * LANES] = own * scale
                return carry

            lax.fori_loop(0, rows, begin, 0)

        @pl.when(step == last - 1)
        def _():
            extra(True)

        @pl.when(jnp.logical_and(step >= 2, step < last + 2))
        def _():
            cross_step(step - 2, True)

        @pl.when(step == 3)
        def _():
            for other in range(1, row_count):
                for copy in row_arrivals(lax.rem(r + other, row_count)):
                    copy.wait_recv()
            table = pltpu.make_async_copy(pmeta, ptable, local_sem.at[1])
            table.start()
            table.wait()

        @pl.when(step >= 3)
        def _():
            compute_step(step - 3)

        return carry

    lax.fori_loop(0, last + 3, advance, 0)

    arrive(paired, cross, 1)
    send(SIBLING, paired, cross, 1, True)
    compute(paired, 1)

    def finish(i, carry):
        for w in range(2):
            out_ref[i, w] = (-0.5 * acc[i, :, w * LANES:(w + 1) * LANES]).astype(out_ref.dtype)
        return carry

    lax.fori_loop(0, rows, finish, 0)

    def drain(step, carry):
        line_step(step, False)
        cross_step(step, False)
        return carry

    lax.fori_loop(0, last, drain, 0)
    extra(False)
    send(SIBLING, paired, cross, 1, False)
    for other in range(1, row_count):
        for copy in row_copies(lax.rem(r + other, row_count)):
            copy.wait_send()


def shards(row_count, col_count, y_blocks, y_cols, prod_blocks, prod_cols, out_cols):
    rows, _, size, _ = y_blocks.shape

    def lane_rows(cols):
        table = jnp.concatenate([cols.reshape(1, rows), cols.reshape(1, rows) % rows], axis=0)
        return jnp.pad(table, ((0, 6), (0, LANES - rows)))

    anywhere = pl.BlockSpec(memory_space=pl.ANY)
    scalars = pl.BlockSpec(memory_space=pltpu.SMEM)
    dma = pltpu.SemaphoreType.DMA
    y_next = pl.pallas_call(
        functools.partial(kernel, row_count, col_count),
        out_shape=jax.ShapeDtypeStruct((rows, 2, size, size), jnp.bfloat16),
        in_specs=[anywhere] * 4 + [scalars] * 2,
        out_specs=pl.BlockSpec(memory_space=pltpu.VMEM),
        scratch_shapes=[
            pltpu.VMEM((col_count, 4, rows, size, size), jnp.bfloat16),
            pltpu.VMEM((row_count * rows + 1, size, size), jnp.bfloat16),
            pltpu.VMEM((rows, size, 2 * size), jnp.float32),
            pltpu.VMEM((col_count, 4, 8, LANES), jnp.int32),
            pltpu.VMEM((row_count, 8, LANES), jnp.int32),
            pltpu.SMEM((col_count, 4, 8, LANES), jnp.int32),
            pltpu.SMEM((row_count, 8, LANES), jnp.int32),
            dma((4, col_count, 4, 2)),
            dma((col_count, 4, 2)),
            dma((4, col_count, 4)),
            dma((col_count, 4)),
            dma((row_count,)),
            dma((row_count,)),
            dma((row_count,)),
            dma((row_count,)),
            dma((4,)),
        ],
        compiler_params=pltpu.CompilerParams(
            collective_id=0, has_side_effects=True, vmem_limit_bytes=56 * 1024 * 1024
        ),
    )(
        y_blocks.reshape(rows, size, size), prod_blocks.reshape(rows, size, size),
        lane_rows(y_cols), lane_rows(prod_cols), y_cols.reshape(rows), out_cols.reshape(2 * rows),
    )
    return y_next.reshape(rows, 1, 2, size, size)


def solution(mesh):
    placed = (
        P("rows", ("cols", "layers"), None, None),
        P("rows", ("cols", "layers")),
        P("rows", ("cols", "layers"), None, None),
        P("rows", ("cols", "layers")),
        P("rows", ("cols", "layers"), None),
    )
    return jax.shard_map(
        functools.partial(shards, mesh.shape["rows"], mesh.shape["cols"]),
        mesh=mesh,
        in_specs=placed,
        out_specs=P("rows", ("cols", "layers"), None, None, None),
        check_vma=False,
    )
```

time: 465 us -> 160 us (0.34)
  Pallas kernels: 0 us -> 149 us
  waiting for transfers between devices: 149 us -> 0 us
  other arithmetic: 106 us -> 2.66 us
  local copies, waits for them, and re-layouts: 96.5 us -> 6.58 us
  matrix products: 69.3 us -> 0 us
  blocking collectives: 27.2 us -> 0 us
  between operations: 14.1 us -> 0.01 us
    pallas_call x0 -> x1, Pallas kernels: none -> 149 us  [shards(): pl.pallas_call(functools.partial(kernel, row_count, col_count), out_shape...]
    all_gather x2 -> x0, waiting for transfers between devices: 148 us -> none  [the longest x1 130 us: shards(): lax.all_gather(y_blocks, ('cols', 'layers'), axis=1, tiled=True)]
    add x16 -> x0, other arithmetic: 98 us -> none  [advance(): return summed + weighted]
    dot_general x16 -> x0, matrix products: 69.3 us -> none  [advance(): jnp.einsum('igab,igtbc->igtac', left_blocks, right_blocks, preferred_elem...]
    gather x32 -> x0, local copies, waits for them, and re-layouts: 56.3 us -> none  [the longest x16 43.8 us: advance(): right_blocks = lookup[lookup_rows]]
    mul x16 -> x0, local copies, waits for them, and re-layouts: 38 us -> none  [advance(): products[:, :, :, None] * present[..., None, None]]
    all_gather x1 -> x0, blocking collectives: 22 us -> none  [shards(): lax.all_gather(y_cols, ('cols', 'layers'), axis=1, tiled=True)]
    convert_element_type x18 -> x0, other arithmetic: 7.61 us -> none  [the longest x1 5.51 us: shards(): return updated.astype(jnp.bfloat16)]
  transfers between devices with their start and end apart: 2 -> 0, of which waited for: 2 -> 0; matrix products, arithmetic and copies ran while one was open for 1% -> 0% of each run, Pallas kernels for 0% -> 0%
where the time goes in v1:
time: 160 us; the launch traced here: 158 us
  Pallas kernels  149 us (93%)
  local copies, waits for them, and re-layouts  6.58 us (4%)
  other arithmetic  2.66 us (2%)
    pallas_call x1, Pallas kernels, shards(): pl.pallas_call(functools.partial(kernel, row_count, col_count), out_shape...  149 us
    unnamed x2, local copies, waits for them, and re-layouts  4.73 us

profile of v1, /device:TPU:0, one launch (start us, length us, event | category | flops | bytes accessed | tf_op | source)
XLA Modules:
  0.0 158.0 jit_solution(4530726546792528031)
XLA Ops:
  0.0 0.7 and_select_fusion
  0.7 0.7 pad_add_fusion.1
  1.3 0.7 and_select_fusion.1
  2.0 0.7 pad_add_fusion
  2.7 0.6 pad.7.ymeta_ref
  3.3 0.6 pad.8.pmeta_ref
  3.9 0.8 copy.8
  4.6 0.6 reshape.92.out_cols_ref
  5.3 148.8 %shard_map.55 = bf16[48,2,128,128]{3,2,1,0:T(8,128)(2,1)} custom-call(bf16[48,128,128]{2,1,0:T(8,128)(2,1)} %bitcast.13, bf16[48,128,128]{2,1,0:T(8,128)(2,1)} %bitcast.14, s32[8,128]{1,0:T(8,128)} %pad.7.ymeta_ref, s32[8,128]{1,0:T(8,128)} %pad.8.pmeta_ref, s32[48]{0:T(128)} %bitcast.16, s32[96]{0:T(128)} %reshape.92.out_cols_ref), custom_call_target="tpu_custom_call" | custom-call | tf_op jit(solution)/shard_map/pallas_call | solution.py:307
  154.0 4.0 %copy.11 = bf16[48,1,2,128,128]{4,3,2,1,0:T(8,128)(2,1)} copy(bf16[48,1,2,128,128]{4,3,2,1,0:T(8,128)(2,1)} %bitcast.12) | data formatting | bytes 6291456

commit v2 on v1

v2 whole, which is shorter than its diff:
```python
import functools

import jax
import jax.numpy as jnp
from jax import lax
from jax.experimental import pallas as pl
from jax.experimental.pallas import tpu as pltpu
from jax.sharding import PartitionSpec as P

TILE_COLS = 6
LANES = 128
PARTS = 4
TOGETHER = 3
MESH = pl.DeviceIdType.MESH
UP, DOWN, CROSS, SIBLING = range(4)


def kernel(
    row_count, col_count, y_ref, m_ref, table_ref, out_ref,
    yall, mall, acc, ytables, rtables, ytable, rtable,
    send_sem, recv_sem, tsend_sem, trecv_sem, row_send, row_recv, rtable_send, rtable_recv, local_sem,
):
    rows = y_ref.shape[0]
    piece = rows // PARTS
    r, z, l = lax.axis_index("rows"), lax.axis_index("cols"), lax.axis_index("layers")
    cross = lax.rem(l + 2, 4)
    sibling = l + 1 - 2 * lax.rem(l, 2)
    cross_sibling = lax.rem(sibling + 2, 4)
    paired = z + 1 - 2 * lax.rem(z, 2)
    targets = {UP: (r, z + 1, l), DOWN: (r, z - 1, l), CROSS: (r, z, cross), SIBLING: (r, z, sibling)}

    own_copies = [
        pltpu.make_async_copy(y_ref, yall.at[z, l], local_sem.at[0]),
        pltpu.make_async_copy(m_ref, mall.at[pl.ds(r * rows, rows)], local_sem.at[1]),
        pltpu.make_async_copy(table_ref, ytables.at[z, l], local_sem.at[2]),
        pltpu.make_async_copy(table_ref, rtables.at[r], local_sem.at[3]),
        pltpu.make_async_copy(table_ref, rtable.at[row_count], local_sem.at[4]),
    ]
    for copy in own_copies:
        copy.start()

    barrier = pltpu.get_barrier_semaphore()

    def greet(device):
        pl.semaphore_signal(barrier, inc=1, device_id=device, device_id_type=MESH)

    greet(targets[CROSS])
    greet(targets[SIBLING])
    for step in range(1, row_count):
        greet((lax.rem(r + step, row_count), z, l))

    @pl.when(z + 1 < col_count)
    def _():
        greet(targets[UP])

    @pl.when(z > 0)
    def _():
        greet(targets[DOWN])

    line_peers = jnp.where(z > 0, 1, 0) + jnp.where(z + 1 < col_count, 1, 0)
    pl.semaphore_wait(barrier, 1 + row_count + line_peers)

    for copy in own_copies:
        copy.wait()

    def chunk_copy(way, at, tile, part, device):
        return pltpu.make_async_remote_copy(
            src_ref=yall.at[at, tile, pl.ds(part * piece, piece)],
            dst_ref=yall.at[at, tile, pl.ds(part * piece, piece)],
            send_sem=send_sem.at[way, at, tile, part],
            recv_sem=recv_sem.at[at, tile, part],
            device_id=device,
            device_id_type=MESH,
        )

    def table_copy(way, at, tile, device):
        return pltpu.make_async_remote_copy(
            src_ref=ytables.at[at, tile],
            dst_ref=ytables.at[at, tile],
            send_sem=tsend_sem.at[way, at, tile],
            recv_sem=trecv_sem.at[at, tile],
            device_id=device,
            device_id_type=MESH,
        )

    def send(way, at, tile, part, start, device=None):
        device = targets[way] if device is None else device
        chunk = chunk_copy(way, at, tile, part, device)
        if start:
            chunk.start()
        else:
            chunk.wait_send()

        @pl.when(part == 0)
        def _():
            table = table_copy(way, at, tile, device)
            if start:
                table.start()
            else:
                table.wait_send()

    def arrive(at, tile, part):
        chunk_copy(SIBLING, at, tile, part, targets[SIBLING]).wait_recv()

        @pl.when(part == 0)
        def _():
            table_copy(SIBLING, at, tile, targets[SIBLING]).wait_recv()

    def origins(step):
        away, part = step // PARTS, lax.rem(step, PARTS)
        return away, part, ((z - away, z - away >= 0), (z + away, jnp.logical_and(z + away < col_count, away > 0)))

    def by_cross_link(at, part):
        return jnp.logical_not(jnp.logical_and(at == paired, part >= PARTS // 2))

    def line_step(step, start):
        away, part, sides = origins(step)
        for side, (at, valid) in enumerate(sides):
            @pl.when(valid)
            def _():
                if start:
                    @pl.when(away > 0)
                    def _():
                        arrive(at, l, part)

                if side == 0:
                    @pl.when(z + 1 < col_count)
                    def _():
                        send(UP, at, l, part, start)

                @pl.when(jnp.logical_and(z > 0, (away == 0) if side == 0 else True))
                def _():
                    send(DOWN, at, l, part, start)

                @pl.when(by_cross_link(at, part))
                def _():
                    send(CROSS, at, l, part, start)

                send(SIBLING, at, l, part, start)

    def cross_step(step, start):
        away, part, sides = origins(step)
        for at, valid in sides:
            @pl.when(jnp.logical_and(valid, by_cross_link(at, part)))
            def _():
                if start:
                    arrive(at, cross, part)
                send(SIBLING, at, cross, part, start)

    def compute(at, part, mine, other):
        arrive(at, other, part)

        @pl.when(part == 0)
        def _():
            copies = [
                pltpu.make_async_copy(ytables.at[at, tile], ytable.at[at, tile], local_sem.at[n])
                for n, tile in enumerate((mine, other))
            ]
            for copy in copies:
                copy.start()
            for copy in copies:
                copy.wait()

        def some_rows(j, carry):
            sums = []
            for u in range(TOGETHER):
                i = part * piece + j * TOGETHER + u
                wanted = [rtable[row_count, 3, i], rtable[row_count, 4, i]]
                left, right = [], []
                for tile in (mine, other):
                    left.append(yall[at, tile, i])
                    first = TILE_COLS * (at * 4 + tile)
                    inner = ytable[at, tile, 0, i]
                    found = rtable[first // rows, 2, ytable[at, tile, 1, i]]
                    right.append(jnp.concatenate(
                        [mall[jnp.where(found == want, inner, row_count * rows)] for want in wanted], axis=1
                    ))
                sums.append(acc[i] + jnp.dot(
                    jnp.concatenate(left, axis=1), jnp.concatenate(right, axis=0),
                    preferred_element_type=jnp.float32,
                ))
            for u in range(TOGETHER):
                acc[part * piece + j * TOGETHER + u] = sums[u]
            return carry

        lax.fori_loop(0, piece // TOGETHER, some_rows, 0)

    def compute_line(step, carry):
        away, part, sides = origins(step)
        for at, valid in sides:
            @pl.when(valid)
            def _():
                compute(at, part, l, sibling)
        return carry

    def compute_cross(step, carry):
        away, part, sides = origins(step)
        for at, valid in sides:
            @pl.when(jnp.logical_and(valid, by_cross_link(at, part)))
            def _():
                compute(at, part, cross, cross_sibling)
        return carry

    def row_copies(owner, other):
        device = (other, z, l)
        owned = pl.ds(owner * rows, rows)
        key = jnp.where(owner == r, other, owner)
        blocks = pltpu.make_async_remote_copy(
            src_ref=mall.at[owned],
            dst_ref=mall.at[owned],
            send_sem=row_send.at[key],
            recv_sem=row_recv.at[owner],
            device_id=device,
            device_id_type=MESH,
        )
        table = pltpu.make_async_remote_copy(
            src_ref=rtables.at[owner],
            dst_ref=rtables.at[owner],
            send_sem=rtable_send.at[key],
            recv_sem=rtable_recv.at[owner],
            device_id=device,
            device_id_type=MESH,
        )
        return blocks, table

    def extra(part, start):
        send(UP, z, cross, part, start, (r, paired, l))

    last = PARTS * col_count
    first_sums = last // 2
    lag = PARTS + 1

    def advance(step, carry):
        @pl.when(step < last)
        def _():
            line_step(step, True)

        @pl.when(step == 0)
        def _():
            for other in range(1, row_count):
                for copy in row_copies(r, lax.rem(r + other, row_count)):
                    copy.start()
            mall[row_count * rows] = jnp.zeros(mall.shape[1:], mall.dtype)

            def begin(i, carry):
                own = yall[z, l, i].astype(jnp.float32)
                for w in range(2):
                    scale = jnp.where(rtable[row_count, 3 + w, i] == rtable[row_count, 0, i], -3.0, 0.0)
                    acc[i, :, w * LANES:(w + 1) * LANES] = own * scale
                return carry

            lax.fori_loop(0, rows, begin, 0)

        @pl.when(step == last - 1)
        def _():
            for part in range(PARTS // 2, PARTS):
                extra(part, True)

        @pl.when(jnp.logical_and(step >= lag, step < last + lag))
        def _():
            cross_step(step - lag, True)

        @pl.when(step == first_sums)
        def _():
            for n in range(1, row_count):
                other = lax.rem(r + n, row_count)
                for copy in row_copies(other, other):
                    copy.wait_recv()
            copies = [pltpu.make_async_copy(rtables.at[n], rtable.at[n], local_sem.at[n]) for n in range(row_count)]
            for copy in copies:
                copy.start()
            for copy in copies:
                copy.wait()

        def reached(behind, now):
            return jnp.clip(jnp.minimum(now - behind, 2 * (now - first_sums + 1)), 0, last)

        lax.fori_loop(reached(0, step - 1), reached(0, step), compute_line, 0)
        lax.fori_loop(reached(lag, step - 1), reached(lag, step), compute_cross, 0)
        return carry

    lax.fori_loop(0, last + lag + 1, advance, 0)

    for part in range(PARTS // 2, PARTS):
        arrive(paired, cross, part)
        send(SIBLING, paired, cross, part, True)

    def compute_extra(part, carry):
        compute(paired, part, cross, cross_sibling)
        return carry

    lax.fori_loop(PARTS // 2, PARTS, compute_extra, 0)

    def finish(i, carry):
        for w in range(2):
            out_ref[i, w] = (-0.5 * acc[i, :, w * LANES:(w + 1) * LANES]).astype(out_ref.dtype)
        return carry

    lax.fori_loop(0, rows, finish, 0)

    def drain(step, carry):
        line_step(step, False)
        cross_step(step, False)
        return carry

    lax.fori_loop(0, last, drain, 0)
    for part in range(PARTS // 2, PARTS):
        extra(part, False)
        send(SIBLING, paired, cross, part, False)
    for n in range(1, row_count):
        for copy in row_copies(r, lax.rem(r + n, row_count)):
            copy.wait_send()


def shards(row_count, col_count, y_blocks, y_cols, prod_blocks, prod_cols, out_cols):
    rows, _, size, _ = y_blocks.shape
    table = jnp.concatenate([y_cols, y_cols % rows, prod_cols, out_cols[:, 0]], axis=1)
    table = jnp.pad(table, ((0, LANES - rows), (0, 3))).T
    anywhere = pl.BlockSpec(memory_space=pl.ANY)
    dma = pltpu.SemaphoreType.DMA
    y_next = pl.pallas_call(
        functools.partial(kernel, row_count, col_count),
        out_shape=jax.ShapeDtypeStruct((rows, 2, size, size), jnp.bfloat16),
        in_specs=[anywhere] * 3,
        out_specs=pl.BlockSpec(memory_space=pltpu.VMEM),
        scratch_shapes=[
            pltpu.VMEM((col_count, 4, rows, size, size), jnp.bfloat16),
            pltpu.VMEM((row_count * rows + 1, size, size), jnp.bfloat16),
            pltpu.VMEM((rows, size, 2 * size), jnp.float32),
            pltpu.VMEM((col_count, 4, 8, LANES), jnp.int32),
            pltpu.VMEM((row_count, 8, LANES), jnp.int32),
            pltpu.SMEM((col_count, 4, 8, LANES), jnp.int32),
            pltpu.SMEM((row_count + 1, 8, LANES), jnp.int32),
            dma((4, col_count, 4, PARTS)),
            dma((col_count, 4, PARTS)),
            dma((4, col_count, 4)),
            dma((col_count, 4)),
            dma((row_count,)),
            dma((row_count,)),
            dma((row_count,)),
            dma((row_count,)),
            dma((max(5, row_count),)),
        ],
        compiler_params=pltpu.CompilerParams(
            collective_id=0, has_side_effects=True, vmem_limit_bytes=56 * 1024 * 1024
        ),
    )(y_blocks.reshape(rows, size, size), prod_blocks.reshape(rows, size, size), table)
    return y_next.reshape(rows, 1, 2, size, size)


def solution(mesh):
    placed = (
        P("rows", ("cols", "layers"), None, None),
        P("rows", ("cols", "layers")),
        P("rows", ("cols", "layers"), None, None),
        P("rows", ("cols", "layers")),
        P("rows", ("cols", "layers"), None),
    )
    return jax.shard_map(
        functools.partial(shards, mesh.shape["rows"], mesh.shape["cols"]),
        mesh=mesh,
        in_specs=placed,
        out_specs=P("rows", ("cols", "layers"), None, None, None),
        check_vma=False,
    )
```

time: 160 us -> 143 us (0.89); the launches traced: 158 us -> 143 us
  Pallas kernels: 149 us -> 137 us
  local copies, waits for them, and re-layouts: 6.58 us -> 4.57 us
    pallas_call x1, Pallas kernels: 149 us -> 137 us  [shards(): pl.pallas_call(functools.partial(kernel, row_count, col_count), out_shape...]
    unnamed x2 -> x1, local copies, waits for them, and re-layouts: 4.73 us -> 3.97 us
where the time goes in v2:
time: 143 us
  Pallas kernels  137 us (96%)
  local copies, waits for them, and re-layouts  4.57 us (3%)
    pallas_call x1, Pallas kernels, shards(): pl.pallas_call(functools.partial(kernel, row_count, col_count), out_shape...  137 us
    unnamed x1, local copies, waits for them, and re-layouts  3.97 us

profile of v2, /device:TPU:0, one launch (start us, length us, event | category | flops | bytes accessed | tf_op | source)
XLA Modules:
  0.0 142.8 jit_solution(10121363721819249789)
XLA Ops:
  0.0 0.7 and_select_fusion
  0.7 0.7 pad_add_fusion
  1.4 0.6 pad_bitcast_fusion.table_ref
  2.0 136.8 %shard_map.55 = bf16[48,2,128,128]{3,2,1,0:T(8,128)(2,1)} custom-call(bf16[48,128,128]{2,1,0:T(8,128)(2,1)} %bitcast.9, bf16[48,128,128]{2,1,0:T(8,128)(2,1)} %bitcast.10, s32[8,128]{1,0:T(8,128)} %pad_bitcast_fusion.table_ref), custom_call_target="tpu_custom_call" | custom-call | tf_op jit(solution)/shard_map/pallas_call | solution.py:321
  138.8 4.0 %copy.8 = bf16[48,1,2,128,128]{4,3,2,1,0:T(8,128)(2,1)} copy(bf16[48,1,2,128,128]{4,3,2,1,0:T(8,128)(2,1)} %bitcast.8) | data formatting | bytes 6291456

commit v3 on v2

--- a/solution.py
+++ b/solution.py
@@ -9,7 +9,7 @@
 
 TILE_COLS = 6
 LANES = 128
-PARTS = 4
+PARTS = 8
 TOGETHER = 3
 MESH = pl.DeviceIdType.MESH
 UP, DOWN, CROSS, SIBLING = range(4)
@@ -17,8 +17,8 @@
 
 def kernel(
     row_count, col_count, y_ref, m_ref, table_ref, out_ref,
-    yall, mall, acc, ytables, rtables, ytable, rtable,
-    send_sem, recv_sem, tsend_sem, trecv_sem, row_send, row_recv, rtable_send, rtable_recv, local_sem,
+    yall, mall, acc, outs, ytables, rtables, ytable, rtable,
+    send_sem, recv_sem, tsend_sem, trecv_sem, row_send, row_recv, rtable_send, rtable_recv, local_sem, out_sem,
 ):
     rows = y_ref.shape[0]
     piece = rows // PARTS
@@ -251,7 +251,7 @@
 
             lax.fori_loop(0, rows, begin, 0)
 
-        @pl.when(step == last - 1)
+        @pl.when(step == PARTS * (jnp.maximum(z, col_count - 1 - z) + 1) - 1)
         def _():
             for part in range(PARTS // 2, PARTS):
                 extra(part, True)
@@ -281,22 +281,37 @@
 
     lax.fori_loop(0, last + lag + 1, advance, 0)
 
-    for part in range(PARTS // 2, PARTS):
-        arrive(paired, cross, part)
-        send(SIBLING, paired, cross, part, True)
-
-    def compute_extra(part, carry):
-        compute(paired, part, cross, cross_sibling)
-        return carry
-
-    lax.fori_loop(PARTS // 2, PARTS, compute_extra, 0)
-
-    def finish(i, carry):
-        for w in range(2):
-            out_ref[i, w] = (-0.5 * acc[i, :, w * LANES:(w + 1) * LANES]).astype(out_ref.dtype)
-        return carry
-
-    lax.fori_loop(0, rows, finish, 0)
+    def out_copy(part):
+        some = pl.ds(part * piece, piece)
+        return pltpu.make_async_copy(outs.at[some], out_ref.at[some], out_sem.at[part])
+
+    def finish(part, carry):
+        def one_row(j, carry):
+            i = part * piece + j
+            for w in range(2):
+                outs[i, w] = (-0.5 * acc[i, :, w * LANES:(w + 1) * LANES]).astype(outs.dtype)
+            return carry
+
+        lax.fori_loop(0, piece, one_row, 0)
+        out_copy(part).start()
+        return carry
+
+    lax.fori_loop(0, PARTS // 2, finish, 0)
+
+    def close(part, carry):
+        @pl.when(part < PARTS)
+        def _():
+            arrive(paired, cross, part)
+            send(SIBLING, paired, cross, part, True)
+
+        @pl.when(part > PARTS // 2)
+        def _():
+            compute(paired, part - 1, cross, cross_sibling)
+            finish(part - 1, 0)
+
+        return carry
+
+    lax.fori_loop(PARTS // 2, PARTS + 1, close, 0)
 
     def drain(step, carry):
         line_step(step, False)
@@ -310,6 +325,8 @@
     for n in range(1, row_count):
         for copy in row_copies(r, lax.rem(r + n, row_count)):
             copy.wait_send()
+    for part in range(PARTS):
+        out_copy(part).wait()
 
 
 def shards(row_count, col_count, y_blocks, y_cols, prod_blocks, prod_cols, out_cols):
@@ -322,11 +339,12 @@
         functools.partial(kernel, row_count, col_count),
         out_shape=jax.ShapeDtypeStruct((rows, 2, size, size), jnp.bfloat16),
         in_specs=[anywhere] * 3,
-        out_specs=pl.BlockSpec(memory_space=pltpu.VMEM),
+        out_specs=anywhere,
         scratch_shapes=[
             pltpu.VMEM((col_count, 4, rows, size, size), jnp.bfloat16),
             pltpu.VMEM((row_count * rows + 1, size, size), jnp.bfloat16),
             pltpu.VMEM((rows, size, 2 * size), jnp.float32),
+            pltpu.VMEM((rows, 2, size, size), jnp.bfloat16),
             pltpu.VMEM((col_count, 4, 8, LANES), jnp.int32),
             pltpu.VMEM((row_count, 8, LANES), jnp.int32),
             pltpu.SMEM((col_count, 4, 8, LANES), jnp.int32),
@@ -340,6 +358,7 @@
             dma((row_count,)),
             dma((row_count,)),
             dma((max(5, row_count),)),
+            dma((PARTS,)),
         ],
         compiler_params=pltpu.CompilerParams(
             collective_id=0, has_side_effects=True, vmem_limit_bytes=56 * 1024 * 1024

time: 143 us -> 145 us (1.014)
    pallas_call x1, Pallas kernels: 137 us -> 138 us  [shards(): pl.pallas_call(functools.partial(kernel, row_count, col_count), out_shape...]
where the time goes in v3:
time: 145 us; the launch traced here: 144 us
  Pallas kernels  138 us (95%)
  local copies, waits for them, and re-layouts  4.57 us (3%)
    pallas_call x1, Pallas kernels, shards(): pl.pallas_call(functools.partial(kernel, row_count, col_count), out_shape...  138 us
    unnamed x1, local copies, waits for them, and re-layouts  3.97 us

profile of v3, /device:TPU:0, one launch (start us, length us, event | category | flops | bytes accessed | tf_op | source)
XLA Modules:
  0.0 144.3 jit_solution(6647655097069463740)
XLA Ops:
  0.0 0.7 and_select_fusion
  0.7 0.7 pad_add_fusion
  1.4 0.6 pad_bitcast_fusion.table_ref
  2.0 138.3 %shard_map.55 = bf16[48,2,128,128]{3,2,1,0:T(8,128)(2,1)} custom-call(bf16[48,128,128]{2,1,0:T(8,128)(2,1)} %bitcast.9, bf16[48,128,128]{2,1,0:T(8,128)(2,1)} %bitcast.10, s32[8,128]{1,0:T(8,128)} %pad_bitcast_fusion.table_ref), custom_call_target="tpu_custom_call" | custom-call | tf_op jit(solution)/shard_map/pallas_call | solution.py:338
  140.3 4.0 %copy.8 = bf16[48,1,2,128,128]{4,3,2,1,0:T(8,128)(2,1)} copy(bf16[48,1,2,128,128]{4,3,2,1,0:T(8,128)(2,1)} %bitcast.8) | data formatting | bytes 6291456

commit v4 on v3

--- a/solution.py
+++ b/solution.py
@@ -10,6 +10,7 @@
 TILE_COLS = 6
 LANES = 128
 PARTS = 8
+WINDOW = 2
 TOGETHER = 3
 MESH = pl.DeviceIdType.MESH
 UP, DOWN, CROSS, SIBLING = range(4)
@@ -231,6 +232,10 @@
     lag = PARTS + 1
 
     def advance(step, carry):
+        @pl.when(jnp.logical_and(step >= WINDOW, step < PARTS))
+        def _():
+            line_step(step - WINDOW, False)
+
         @pl.when(step < last)
         def _():
             line_step(step, True)
@@ -251,7 +256,7 @@
 
             lax.fori_loop(0, rows, begin, 0)
 
-        @pl.when(step == PARTS * (jnp.maximum(z, col_count - 1 - z) + 1) - 1)
+        @pl.when(step == last - 5)
         def _():
             for part in range(PARTS // 2, PARTS):
                 extra(part, True)
@@ -314,7 +319,10 @@
     lax.fori_loop(PARTS // 2, PARTS + 1, close, 0)
 
     def drain(step, carry):
-        line_step(step, False)
+        @pl.when(step >= PARTS - WINDOW)
+        def _():
+            line_step(step, False)
+
         cross_step(step, False)
         return carry
 

time: 145 us -> 145 us (level)
  no operation moved by 1% of the time
where the time goes in v4:
time: 145 us; the launch traced here: 144 us
  Pallas kernels  138 us (95%)
  local copies, waits for them, and re-layouts  4.57 us (3%)
    pallas_call x1, Pallas kernels, shards(): pl.pallas_call(functools.partial(kernel, row_count, col_count), out_shape...  138 us
    unnamed x1, local copies, waits for them, and re-layouts  3.97 us

profile of v4, /device:TPU:0, one launch (start us, length us, event | category | flops | bytes accessed | tf_op | source)
XLA Modules:
  0.0 144.3 jit_solution(13738203337580933486)
XLA Ops:
  0.0 0.7 and_select_fusion
  0.7 0.7 pad_add_fusion
  1.4 0.6 pad_bitcast_fusion.table_ref
  2.0 138.4 %shard_map.55 = bf16[48,2,128,128]{3,2,1,0:T(8,128)(2,1)} custom-call(bf16[48,128,128]{2,1,0:T(8,128)(2,1)} %bitcast.9, bf16[48,128,128]{2,1,0:T(8,128)(2,1)} %bitcast.10, s32[8,128]{1,0:T(8,128)} %pad_bitcast_fusion.table_ref), custom_call_target="tpu_custom_call" | custom-call | tf_op jit(solution)/shard_map/pallas_call | solution.py:346
  140.4 4.0 %copy.8 = bf16[48,1,2,128,128]{4,3,2,1,0:T(8,128)(2,1)} copy(bf16[48,1,2,128,128]{4,3,2,1,0:T(8,128)(2,1)} %bitcast.8) | data formatting | bytes 6291456

commit v5 on v4

--- a/solution.py
+++ b/solution.py
@@ -9,9 +9,9 @@
 
 TILE_COLS = 6
 LANES = 128
-PARTS = 8
-WINDOW = 2
-TOGETHER = 3
+PARTS = 4
+WINDOW = 4
+TOGETHER = 2
 MESH = pl.DeviceIdType.MESH
 UP, DOWN, CROSS, SIBLING = range(4)
 
@@ -148,14 +148,15 @@
                     arrive(at, cross, part)
                 send(SIBLING, at, cross, part, start)
 
-    def compute(at, part, mine, other):
-        arrive(at, other, part)
+    def compute(at, part, tiles, awaited):
+        for tile in awaited:
+            arrive(at, tile, part)
 
         @pl.when(part == 0)
         def _():
             copies = [
                 pltpu.make_async_copy(ytables.at[at, tile], ytable.at[at, tile], local_sem.at[n])
-                for n, tile in enumerate((mine, other))
+                for n, tile in enumerate(tiles)
             ]
             for copy in copies:
                 copy.start()
@@ -168,7 +169,7 @@
                 i = part * piece + j * TOGETHER + u
                 wanted = [rtable[row_count, 3, i], rtable[row_count, 4, i]]
                 left, right = [], []
-                for tile in (mine, other):
+                for tile in tiles:
                     left.append(yall[at, tile, i])
                     first = TILE_COLS * (at * 4 + tile)
                     inner = ytable[at, tile, 0, i]
@@ -186,20 +187,27 @@
 
         lax.fori_loop(0, piece // TOGETHER, some_rows, 0)
 
+    def fused(at, away, part):
+        return jnp.logical_and(by_cross_link(at, part), away <= 1)
+
     def compute_line(step, carry):
         away, part, sides = origins(step)
         for at, valid in sides:
-            @pl.when(valid)
+            @pl.when(jnp.logical_and(valid, jnp.logical_not(fused(at, away, part))))
             def _():
-                compute(at, part, l, sibling)
+                compute(at, part, (l, sibling), (sibling,))
         return carry
 
     def compute_cross(step, carry):
         away, part, sides = origins(step)
         for at, valid in sides:
-            @pl.when(jnp.logical_and(valid, by_cross_link(at, part)))
+            @pl.when(jnp.logical_and(valid, fused(at, away, part)))
             def _():
-                compute(at, part, cross, cross_sibling)
+                compute(at, part, (l, sibling, cross, cross_sibling), (sibling, cross_sibling))
+
+            @pl.when(jnp.logical_and(valid, jnp.logical_and(by_cross_link(at, part), away > 1)))
+            def _():
+                compute(at, part, (cross, cross_sibling), (cross_sibling,))
         return carry
 
     def row_copies(owner, other):
@@ -256,7 +264,7 @@
 
             lax.fori_loop(0, rows, begin, 0)
 
-        @pl.when(step == last - 5)
+        @pl.when(step == last - 3)
         def _():
             for part in range(PARTS // 2, PARTS):
                 extra(part, True)
@@ -311,7 +319,7 @@
 
         @pl.when(part > PARTS // 2)
         def _():
-            compute(paired, part - 1, cross, cross_sibling)
+            compute(paired, part - 1, (cross, cross_sibling), (cross_sibling,))
             finish(part - 1, 0)
 
         return carry

time: 145 us -> 143 us (0.986)
    pallas_call x1, Pallas kernels: 138 us -> 137 us  [shards(): pl.pallas_call(functools.partial(kernel, row_count, col_count), out_shape...]
where the time goes in v5:
time: 143 us; the launch traced here: 142 us
  Pallas kernels  137 us (96%)
  local copies, waits for them, and re-layouts  4.57 us (3%)
    pallas_call x1, Pallas kernels, shards(): pl.pallas_call(functools.partial(kernel, row_count, col_count), out_shape...  137 us
    unnamed x1, local copies, waits for them, and re-layouts  3.97 us

profile of v5, /device:TPU:0, one launch (start us, length us, event | category | flops | bytes accessed | tf_op | source)
XLA Modules:
  0.0 142.5 jit_solution(2105994613136796407)
XLA Ops:
  0.0 0.7 and_select_fusion
  0.7 0.7 pad_add_fusion
  1.4 0.6 pad_bitcast_fusion.table_ref
  2.0 136.5 %shard_map.55 = bf16[48,2,128,128]{3,2,1,0:T(8,128)(2,1)} custom-call(bf16[48,128,128]{2,1,0:T(8,128)(2,1)} %bitcast.9, bf16[48,128,128]{2,1,0:T(8,128)(2,1)} %bitcast.10, s32[8,128]{1,0:T(8,128)} %pad_bitcast_fusion.table_ref), custom_call_target="tpu_custom_call" | custom-call | tf_op jit(solution)/shard_map/pallas_call | solution.py:354
  138.5 4.0 %copy.8 = bf16[48,1,2,128,128]{4,3,2,1,0:T(8,128)(2,1)} copy(bf16[48,1,2,128,128]{4,3,2,1,0:T(8,128)(2,1)} %bitcast.8) | data formatting | bytes 6291456

commit v6 on v5

--- a/solution.py
+++ b/solution.py
@@ -10,7 +10,6 @@
 TILE_COLS = 6
 LANES = 128
 PARTS = 4
-WINDOW = 4
 TOGETHER = 2
 MESH = pl.DeviceIdType.MESH
 UP, DOWN, CROSS, SIBLING = range(4)
@@ -240,10 +239,6 @@
     lag = PARTS + 1
 
     def advance(step, carry):
-        @pl.when(jnp.logical_and(step >= WINDOW, step < PARTS))
-        def _():
-            line_step(step - WINDOW, False)
-
         @pl.when(step < last)
         def _():
             line_step(step, True)
@@ -290,6 +285,15 @@
 
         lax.fori_loop(reached(0, step - 1), reached(0, step), compute_line, 0)
         lax.fori_loop(reached(lag, step - 1), reached(lag, step), compute_cross, 0)
+
+        @pl.when(jnp.logical_and(step >= 2 * PARTS, step < last + 2 * PARTS))
+        def _():
+            line_step(step - 2 * PARTS, False)
+
+        @pl.when(step >= lag + PARTS)
+        def _():
+            cross_step(step - lag - PARTS, False)
+
         return carry
 
     lax.fori_loop(0, last + lag + 1, advance, 0)
@@ -327,14 +331,17 @@
     lax.fori_loop(PARTS // 2, PARTS + 1, close, 0)
 
     def drain(step, carry):
-        @pl.when(step >= PARTS - WINDOW)
+        @pl.when(step >= last + lag + 1 - 2 * PARTS)
         def _():
             line_step(step, False)
 
-        cross_step(step, False)
-        return carry
-
-    lax.fori_loop(0, last, drain, 0)
+        @pl.when(step >= last + 1 - PARTS)
+        def _():
+            cross_step(step, False)
+
+        return carry
+
+    lax.fori_loop(last + 1 - 2 * PARTS, last, drain, 0)
     for part in range(PARTS // 2, PARTS):
         extra(part, False)
         send(SIBLING, paired, cross, part, False)

time: 143 us -> 143 us (level)
  no operation moved by 1% of the time
where the time goes in v6:
time: 143 us; the launch traced here: 142 us
  Pallas kernels  136 us (95%)
  local copies, waits for them, and re-layouts  4.57 us (3%)
    pallas_call x1, Pallas kernels, shards(): pl.pallas_call(functools.partial(kernel, row_count, col_count), out_shape...  136 us
    unnamed x1, local copies, waits for them, and re-layouts  3.97 us

profile of v6, /device:TPU:0, one launch (start us, length us, event | category | flops | bytes accessed | tf_op | source)
XLA Modules:
  0.0 142.3 jit_solution(11456168792248572766)
XLA Ops:
  0.0 0.7 and_select_fusion
  0.7 0.7 pad_add_fusion
  1.4 0.6 pad_bitcast_fusion.table_ref
  2.0 136.3 %shard_map.55 = bf16[48,2,128,128]{3,2,1,0:T(8,128)(2,1)} custom-call(bf16[48,128,128]{2,1,0:T(8,128)(2,1)} %bitcast.9, bf16[48,128,128]{2,1,0:T(8,128)(2,1)} %bitcast.10, s32[8,128]{1,0:T(8,128)} %pad_bitcast_fusion.table_ref), custom_call_target="tpu_custom_call" | custom-call | tf_op jit(solution)/shard_map/pallas_call | solution.py:361
  138.3 4.0 %copy.8 = bf16[48,1,2,128,128]{4,3,2,1,0:T(8,128)(2,1)} copy(bf16[48,1,2,128,128]{4,3,2,1,0:T(8,128)(2,1)} %bitcast.8) | data formatting | bytes 6291456

commit v7 on v6

--- a/solution.py
+++ b/solution.py
@@ -10,6 +10,7 @@
 TILE_COLS = 6
 LANES = 128
 PARTS = 4
+BY_LINE_FROM = 1
 TOGETHER = 2
 MESH = pl.DeviceIdType.MESH
 UP, DOWN, CROSS, SIBLING = range(4)
@@ -111,7 +112,7 @@
         return away, part, ((z - away, z - away >= 0), (z + away, jnp.logical_and(z + away < col_count, away > 0)))
 
     def by_cross_link(at, part):
-        return jnp.logical_not(jnp.logical_and(at == paired, part >= PARTS // 2))
+        return jnp.logical_not(jnp.logical_and(at == paired, part >= BY_LINE_FROM))
 
     def line_step(step, start):
         away, part, sides = origins(step)
@@ -187,7 +188,7 @@
         lax.fori_loop(0, piece // TOGETHER, some_rows, 0)
 
     def fused(at, away, part):
-        return jnp.logical_and(by_cross_link(at, part), away <= 1)
+        return jnp.logical_and(by_cross_link(at, part), away == 0)
 
     def compute_line(step, carry):
         away, part, sides = origins(step)
@@ -204,7 +205,7 @@
             def _():
                 compute(at, part, (l, sibling, cross, cross_sibling), (sibling, cross_sibling))
 
-            @pl.when(jnp.logical_and(valid, jnp.logical_and(by_cross_link(at, part), away > 1)))
+            @pl.when(jnp.logical_and(valid, jnp.logical_and(by_cross_link(at, part), away > 0)))
             def _():
                 compute(at, part, (cross, cross_sibling), (cross_sibling,))
         return carry
@@ -261,7 +262,7 @@
 
         @pl.when(step == last - 3)
         def _():
-            for part in range(PARTS // 2, PARTS):
+            for part in range(BY_LINE_FROM, PARTS):
                 extra(part, True)
 
         @pl.when(jnp.logical_and(step >= lag, step < last + lag))
@@ -313,7 +314,7 @@
         out_copy(part).start()
         return carry
 
-    lax.fori_loop(0, PARTS // 2, finish, 0)
+    lax.fori_loop(0, BY_LINE_FROM, finish, 0)
 
     def close(part, carry):
         @pl.when(part < PARTS)
@@ -321,14 +322,14 @@
             arrive(paired, cross, part)
             send(SIBLING, paired, cross, part, True)
 
-        @pl.when(part > PARTS // 2)
+        @pl.when(part > BY_LINE_FROM)
         def _():
             compute(paired, part - 1, (cross, cross_sibling), (cross_sibling,))
             finish(part - 1, 0)
 
         return carry
 
-    lax.fori_loop(PARTS // 2, PARTS + 1, close, 0)
+    lax.fori_loop(BY_LINE_FROM, PARTS + 1, close, 0)
 
     def drain(step, carry):
         @pl.when(step >= last + lag + 1 - 2 * PARTS)
@@ -342,7 +343,7 @@
         return carry
 
     lax.fori_loop(last + 1 - 2 * PARTS, last, drain, 0)
-    for part in range(PARTS // 2, PARTS):
+    for part in range(BY_LINE_FROM, PARTS):
         extra(part, False)
         send(SIBLING, paired, cross, part, False)
     for n in range(1, row_count):

time: 143 us -> 146 us (1.021)
  Pallas kernels: 136 us -> 140 us
    pallas_call x1, Pallas kernels: 136 us -> 140 us  [shards(): pl.pallas_call(functools.partial(kernel, row_count, col_count), out_shape...]
where the time goes in v7:
time: 146 us
  Pallas kernels  140 us (96%)
  local copies, waits for them, and re-layouts  4.57 us (3%)
    pallas_call x1, Pallas kernels, shards(): pl.pallas_call(functools.partial(kernel, row_count, col_count), out_shape...  140 us
    unnamed x1, local copies, waits for them, and re-layouts  3.97 us

profile of v7, /device:TPU:0, one launch (start us, length us, event | category | flops | bytes accessed | tf_op | source)
XLA Modules:
  0.0 146.0 jit_solution(13255857978530806485)
XLA Ops:
  0.0 0.7 and_select_fusion
  0.7 0.7 pad_add_fusion
  1.4 0.6 pad_bitcast_fusion.table_ref
  2.0 140.1 %shard_map.55 = bf16[48,2,128,128]{3,2,1,0:T(8,128)(2,1)} custom-call(bf16[48,128,128]{2,1,0:T(8,128)(2,1)} %bitcast.9, bf16[48,128,128]{2,1,0:T(8,128)(2,1)} %bitcast.10, s32[8,128]{1,0:T(8,128)} %pad_bitcast_fusion.table_ref), custom_call_target="tpu_custom_call" | custom-call | tf_op jit(solution)/shard_map/pallas_call | solution.py:362
  142.0 4.0 %copy.8 = bf16[48,1,2,128,128]{4,3,2,1,0:T(8,128)(2,1)} copy(bf16[48,1,2,128,128]{4,3,2,1,0:T(8,128)(2,1)} %bitcast.8) | data formatting | bytes 6291456
